TPU v7x, 32 devices: a whole 2x2x4 slice. The times are simulated.
32 devices in a mesh: grp: 2 (over x), lon: 16 (over z, y, core).
Axes of the slice: x: 2, y: 2, z: 4, core: 2. Of those that a mesh axis runs over, the one named last changes fastest.
Arguments:
- field: bfloat16 [128, 256, 512], P('grp', 'lon'), parts along dimension 0, may hold values from -6 to 6
- cotangent: bfloat16 [128, 256, 512], P('grp', 'lon'), parts along dimension 0, may hold values from -6 to 6
- offsets: int32 [64], replicated, may hold values from 0 to 56, as said below
- widths: int32 [64], replicated, may hold values from 2 to 8
- kernel: bfloat16 [64, 8, 5, 3], replicated, may hold values from -1 to 1
- cycle: float32 [6, 8, 3], replicated, may hold values from -2 to 2
- mixing: bfloat16 [512, 3, 512], replicated, may hold values from -0.15625 to 0.15625
Outputs:
- output: bfloat16 [128, 256, 512], P('grp', 'lon'), parts along dimension 0
- field_grad: bfloat16 [128, 256, 512], P('grp', 'lon'), parts along dimension 0
- mixing_grad: float32 [512, 6, 512], P('lon', 'grp'), parts along dimension 1
There are 2 independent parts, one for each index of `grp`. A program takes and returns all parts, laid end to end along the dimension named above; an argument that names none is the same for every part. Nothing has to cross between parts.
Inputs may be any that keep to these rules, and one draw needn't show every extreme that they name: offsets[i] + 8 <= 64; the polar rows i < 6 use all 8 rows.
All inputs are finite; a program needn't handle non-finite values.
Results may differ from a plain program's by a relative error of at most 0.0061.
Values may be sent and summed in bfloat16 or wider, within the bound.
A program may use at most 64 MiB of HBM per device.

v0:
```python
import functools

import jax
import jax.numpy as jnp
from jax import lax
from jax.experimental import pallas as pl
from jax.experimental.pallas import tpu as pltpu
from jax.sharding import PartitionSpec as P

BAND = 8
R = 2
TAPS = 2 * R + 1
K = 3
POLAR = 6
PB = 8
MESH = pl.DeviceIdType.MESH
F32 = jnp.float32
BF16 = jnp.bfloat16


def kernel_body(
    n,
    direct,
    scale,
    field,
    cot_hbm,
    mix_hbm,
    taps,
    offs,
    wids,
    cyc_f,
    cyc_b,
    out,
    fgrad,
    mgrad,
    xt,
    cot,
    mix,
    pieces,
    fwd,
    bwd,
    conv,
    polar,
    mg,
    cg,
    ms,
    zbuf,
    sbuf,
    part,
    partb,
    r1,
    s2,
    r2,
    in_sem,
    h_send,
    h_recv,
    g_send,
    g_recv,
    z_send,
    z_recv,
    s_send,
    s_recv,
    a_send,
    a_recv,
    b_send,
    b_recv,
):
    cols = field.shape[0]
    lat = field.shape[1]
    ch = field.shape[2]
    me = lax.axis_index("lon")
    right, left = lax.rem(me + 1, n), lax.rem(me + n - 1, n)

    barrier = pltpu.get_barrier_semaphore()

    def greet(d, carry):
        pl.semaphore_signal(
            barrier, inc=1, device_id={"lon": lax.rem(me + d, n)}, device_id_type=MESH
        )
        return carry

    lax.fori_loop(1, n, greet, 0)

    load_field = pltpu.make_async_copy(field, xt.at[pl.ds(R, cols)], in_sem.at[0])
    load_mix = pltpu.make_async_copy(mix_hbm, mix, in_sem.at[1])
    load_cot = pltpu.make_async_copy(cot_hbm, cot, in_sem.at[2])
    load_field.start()
    load_mix.start()
    load_cot.start()

    def remote(src, dst, send, recv, peer):
        return pltpu.make_async_remote_copy(
            src_ref=src,
            dst_ref=dst,
            send_sem=send,
            recv_sem=recv,
            device_id={"lon": peer},
            device_id_type=MESH,
        )

    def spread(buf, send, recv):
        def copy(d):
            return remote(buf.at[0], buf.at[d], send.at[d], recv.at[d], lax.rem(me + d, n))

        return copy

    def start_all(copy):
        def step(d, carry):
            copy(d).start()
            return carry

        lax.fori_loop(1, n, step, 0)

    def wait_all(copy):
        def step(d, carry):
            copy(d).wait()
            return carry

        lax.fori_loop(1, n, step, 0)

    pl.semaphore_wait(barrier, n - 1)
    halo_l = remote(
        field.at[pl.ds(0, R)], xt.at[pl.ds(R + cols, R)], h_send.at[0], h_recv.at[0], left
    )
    halo_r = remote(
        field.at[pl.ds(cols - R, R)], xt.at[pl.ds(0, R)], h_send.at[1], h_recv.at[1], right
    )
    halo_l.start()
    halo_r.start()
    load_field.wait()
    zbuf[0] = jnp.sum(xt[R : R + cols, 0:16, :].astype(F32), axis=0)[0:PB]
    zonal_copy = spread(zbuf, z_send, z_recv)
    start_all(zonal_copy)

    wide = 2 * K * lat
    rel = lax.broadcasted_iota(jnp.int32, (lat, wide), 0) - offs[...]
    used = rel < wids[...]
    for t in range(TAPS + 1):
        acc = jnp.zeros((lat, wide), F32)
        for b in range(BAND):
            row = taps[t * BAND + b : t * BAND + b + 1, :]
            acc = jnp.where((rel == b) & used, row, acc)
        pieces[t * lat : (t + 1) * lat, :] = acc
    fwd[...] = pieces[...].T.astype(BF16)
    for a in range(4):
        for p in range(4):
            t = 2 * R - 2 * p + a
            if 0 <= t <= TAPS:
                block = pieces[t * lat : (t + 1) * lat, :].astype(BF16)
            else:
                block = jnp.zeros((lat, wide), BF16)
            bwd[a * lat : (a + 1) * lat, p * wide : (p + 1) * wide] = block

    def conv_pair(p):
        source = xt[pl.ds(2 * p, TAPS + 1)].reshape((TAPS + 1) * lat, ch)
        c = jnp.dot(fwd[...], source, preferred_element_type=F32)
        c = c.reshape(2, K, lat, ch)
        polar[pl.ds(2 * p, 2)] = c[:, :, 0:16]
        conv[pl.ds(2 * p, 2)] = c.astype(BF16)

    def loop(lo, hi, fn):
        def step(i, carry):
            fn(i)
            return carry

        lax.fori_loop(lo, hi, step, 0)

    pairs = cols // 2
    loop(1, pairs - 1, conv_pair)
    halo_l.wait()
    halo_r.wait()
    loop(0, 2, lambda i: conv_pair(i * (pairs - 1)))

    wait_all(zonal_copy)
    zonal = jnp.sum(zbuf[...], axis=0) * scale
    term = jnp.zeros((K * 16, ch), F32)
    for p in range(PB):
        term = term + cyc_f[:, p : p + 1] * zonal[p : p + 1, :]
    term = term.reshape(1, K, 16, ch)
    load_mix.wait()
    load_cot.wait()
    ms[...] = jnp.zeros_like(ms)

    def mix_group(g):
        at = pl.ds(4 * g, 4)
        conv[at, :, 0:16] = (polar[at] + term).astype(BF16)
        mixed = jnp.dot(
            conv[at, 0].reshape(4 * lat, ch), mix[0], preferred_element_type=F32
        )
        for k in range(1, K):
            mixed = mixed + jnp.dot(
                conv[at, k].reshape(4 * lat, ch), mix[k], preferred_element_type=F32
            )
        sig = jax.nn.sigmoid(mixed)
        out[at] = (mixed * sig).astype(BF16).reshape(4, lat, ch)
        ct = cot[at].reshape(4 * lat, ch).astype(F32)
        grad = (ct * (sig * (1.0 + mixed * (1.0 - sig)))).astype(BF16).reshape(4, lat, ch)
        mg[pl.ds(R + 4 * g, 4)] = grad
        ms[...] += jnp.sum(grad[:, 0:16].astype(F32), axis=0)

    groups = cols // 4
    loop(0, 2, lambda i: mix_group(i * (groups - 1)))
    grad_l = remote(
        mg.at[pl.ds(R, R)], mg.at[pl.ds(R + cols, R)], g_send.at[0], g_recv.at[0], left
    )
    grad_r = remote(
        mg.at[pl.ds(cols, R)], mg.at[pl.ds(0, R)], g_send.at[1], g_recv.at[1], right
    )
    grad_l.start()
    grad_r.start()
    loop(1, groups - 1, mix_group)
    sbuf[0] = ms[0:PB]
    sums_copy = spread(sbuf, s_send, s_recv)
    start_all(sums_copy)

    half = ch // 2
    if direct:
        rows = ch // n
        chips = n // 2
        core = lax.rem(me, 2)
        chip = me // 2
        sibling = chip * 2 + (1 - core)
        per = half // (2 * rows)

        def pair_copy(k):
            return remote(
                partb.at[k, 1 - core], r1.at[k], a_send.at[k], a_recv.at[k], sibling
            )

        def chip_copy(k, d):
            return remote(
                s2.at[k, d],
                r2.at[k, d],
                b_send.at[k, d],
                b_recv.at[k, d],
                lax.rem(chip + d, chips) * 2 + core,
            )

        def pass_on(k):
            pair_copy(k).wait()

            def step(d):
                to = lax.rem(chip + d, chips)
                s2[k, d] = (part[k, core, to] + r1[k, to].astype(F32)).astype(BF16)
                chip_copy(k, d).start()

            loop(1, chips, step)

    for k in range(K):

        def product(h):
            lanes = pl.ds(pl.multiple_of(h * half, half), half)
            res = lax.dot_general(
                conv[:, k, :, lanes].reshape(cols * lat, half),
                mg[R : R + cols].reshape(cols * lat, ch),
                (((0,), (0,)), ((), ())),
                preferred_element_type=F32,
            )
            if not direct:
                mgrad[k, lanes, :] = res
                return
            res = res.reshape(per, 2, rows, ch)
            resb = res.astype(BF16)
            for c in range(2):
                part[k, c, pl.ds(h * per, per)] = res[:, c]
                partb[k, c, pl.ds(h * per, per)] = resb[:, c]

        loop(0, 2, product)
        if direct:
            pair_copy(k).start()
            if k > 0:
                pass_on(k - 1)
    if direct:
        pass_on(K - 1)

    def spread_grad(g):
        at = pl.ds(4 * g, 4)
        source = mg[at].reshape(4 * lat, ch)
        for k in range(K):
            res = lax.dot_general(
                source, mix[k], (((1,), (1,)), ((), ())), preferred_element_type=F32
            )
            cg[at, k] = res.astype(BF16).reshape(4, lat, ch)

    loop(1, groups, spread_grad)
    grad_l.wait()
    grad_r.wait()
    loop(0, 2, lambda i: spread_grad(i * groups))

    wait_all(sums_copy)
    total = jnp.sum(sbuf[...], axis=0)
    high = total.astype(BF16)
    low = (total - high.astype(F32)).astype(BF16)
    both = jnp.concatenate([high.astype(F32), low.astype(F32)], axis=0).astype(BF16)
    zgrad = jnp.zeros((PB, ch), F32)
    for k in range(K):
        res = lax.dot_general(
            both, mix[k], (((1,), (1,)), ((), ())), preferred_element_type=F32
        )
        res = res[0:PB] + res[PB : 2 * PB]
        for i in range(POLAR):
            at = k * POLAR + i
            zgrad = zgrad + cyc_b[:, at : at + 1] * res[i : i + 1, :]
    zgrad = zgrad * scale
    zgrad = jnp.concatenate([zgrad, jnp.zeros((16 - PB, ch), F32)], axis=0)[None]

    def field_group(g):
        at = pl.ds(4 * g, 4)
        source = cg[pl.ds(4 * g, 8)].reshape(8 * K * lat, ch)
        res = jnp.dot(bwd[...], source, preferred_element_type=F32).reshape(4, lat, ch)
        fgrad[at] = res.astype(BF16)
        fgrad[at, 0:16] = (res[:, 0:16] + zgrad).astype(BF16)

    loop(0, groups, field_group)

    if direct:
        for k in range(K):
            acc = part[k, core, chip] + r1[k, chip].astype(F32)
            for d in range(1, chips):
                chip_copy(k, d).wait()
                acc = acc + r2[k, d].astype(F32)
            mgrad[k] = acc


def body(n, field, cotangent, offsets, widths, kernel, cycle, mixing):
    lat, cols, ch = field.shape
    scale = float(cols * n) ** (-0.5)
    rows = ch // n
    direct = n % 2 == 0 and n > 2 and rows % 16 == 0
    field_t = jnp.swapaxes(field, 0, 1)
    cot_t = jnp.swapaxes(cotangent, 0, 1)
    mix_t = jnp.swapaxes(mixing, 0, 1)
    taps = jnp.transpose(kernel, (2, 1, 3, 0)).reshape(TAPS * BAND, K * lat).astype(F32)
    taps = jnp.concatenate(
        [jnp.pad(taps, ((0, BAND), (0, 0))), jnp.pad(taps, ((BAND, 0), (0, 0)))], axis=1
    )
    offs = jnp.tile(offsets, 2 * K)[None]
    wids = jnp.tile(widths, 2 * K)[None]
    cyc_f = jnp.pad(jnp.transpose(cycle, (2, 0, 1)), ((0, 0), (0, 16 - POLAR), (0, 0)))
    cyc_f = cyc_f.reshape(K * 16, PB)
    cyc_b = jnp.transpose(cycle, (1, 2, 0)).reshape(PB, K * POLAR)

    wide = 2 * K * lat
    dma = pltpu.SemaphoreType.DMA
    chips = n // 2 if direct else 1
    brows = rows if direct else 16
    vmem = pl.BlockSpec(memory_space=pltpu.VMEM)
    hbm = pl.BlockSpec(memory_space=pl.ANY)
    out_t, fgrad_t, mgrad_t = pl.pallas_call(
        functools.partial(kernel_body, n, direct, scale),
        out_shape=[
            jax.ShapeDtypeStruct((cols, lat, ch), BF16),
            jax.ShapeDtypeStruct((cols, lat, ch), BF16),
            jax.ShapeDtypeStruct((K, rows if direct else ch, ch), F32),
        ],
        in_specs=[hbm] * 3 + [vmem] * 5,
        out_specs=[vmem] * 3,
        scratch_shapes=[
            pltpu.VMEM((cols + 2 * R, lat, ch), BF16),
            pltpu.VMEM((cols, lat, ch), BF16),
            pltpu.VMEM((K, ch, ch), BF16),
            pltpu.VMEM(((TAPS + 1) * lat, wide), F32),
            pltpu.VMEM((wide, (TAPS + 1) * lat), BF16),
            pltpu.VMEM((4 * lat, 4 * wide), BF16),
            pltpu.VMEM((cols, K, lat, ch), BF16),
            pltpu.VMEM((cols, K, 16, ch), F32),
            pltpu.VMEM((cols + 2 * R, lat, ch), BF16),
            pltpu.VMEM((cols + 2 * R, K, lat, ch), BF16),
            pltpu.VMEM((16, ch), F32),
            pltpu.VMEM((n, PB, ch), F32),
            pltpu.VMEM((n, PB, ch), F32),
            pltpu.VMEM((K, 2, chips, brows, ch), F32),
            pltpu.VMEM((K, 2, chips, brows, ch), BF16),
            pltpu.VMEM((K, chips, brows, ch), BF16),
            pltpu.VMEM((K, chips, brows, ch), BF16),
            pltpu.VMEM((K, chips, brows, ch), BF16),
            dma((3,)),
            dma((2,)),
            dma((2,)),
            dma((2,)),
            dma((2,)),
            dma((n,)),
            dma((n,)),
            dma((n,)),
            dma((n,)),
            dma((K,)),
            dma((K,)),
            dma((K, chips)),
            dma((K, chips)),
        ],
        compiler_params=pltpu.CompilerParams(
            collective_id=0, has_side_effects=True, vmem_limit_bytes=56 * 1024 * 1024
        ),
    )(field_t, cot_t, mix_t, taps, offs, wids, cyc_f, cyc_b)
    output = jnp.swapaxes(out_t, 0, 1)
    field_grad = jnp.swapaxes(fgrad_t, 0, 1)
    mixing_grad = jnp.swapaxes(mgrad_t, 0, 1)
    if not direct:
        mixing_grad = lax.psum_scatter(mixing_grad, "lon", scatter_dimension=0, tiled=True)
    return (output, field_grad, mixing_grad)


def solution(mesh):
    in_specs = (P("grp", "lon", None), P("grp", "lon", None), P(), P(), P(), P(), P())
    out_specs = (P("grp", "lon", None), P("grp", "lon", None), P("lon", "grp", None))
    return jax.shard_map(
        functools.partial(body, mesh.shape["lon"]),
        mesh=mesh,
        in_specs=in_specs,
        out_specs=out_specs,
        check_vma=False,
    )
```

profile of v0, /device:TPU:0, one launch (start us, length us, event | category | flops | bytes accessed | tf_op | source)
XLA Modules:
  0.0 62.4 jit_solution(838152261331872028)
XLA Ops:
  0.6 0.7 %tile.4 = s32[6,64]{1,0:T(8,128)S(1)} broadcast(s32[64]{0:T(128)} %param.9), dimensions={1} | broadcast | bytes 1792 | tf_op jit(solution)/shard_map/tile | solution.py:337
  1.3 0.6 %broadcast_in_dim_tile.6.offs = s32[1,384]{1,0:T(1,128)} reshape(s32[6,64]{1,0:T(8,128)S(1)} %tile.4) | data formatting | bytes 3072 | tf_op jit(solution)/shard_map/broadcast_in_dim;tile | solution.py:337
  1.9 0.7 %tile.5 = s32[6,64]{1,0:T(8,128)S(1)} broadcast(s32[64]{0:T(128)} %param.10), dimensions={1} | broadcast | bytes 1792 | tf_op jit(solution)/shard_map/tile | solution.py:338
  2.6 0.7 %broadcast_in_dim_tile.7.wids = s32[1,384]{1,0:T(1,128)} reshape(s32[6,64]{1,0:T(8,128)S(1)} %tile.5) | data formatting | bytes 3072 | tf_op jit(solution)/shard_map/broadcast_in_dim;tile | solution.py:338
  3.3 0.7 %copy.24 = f32[3,6,8]{2,1,0:T(8,128)S(1)} copy(f32[3,6,8]{2,0,1:T(4,128)} %bitcast.18) | data formatting | bytes 1152
  4.0 0.6 pad.14.clone
  4.6 0.8 %copy.21 = f32[8,3,6]{2,1,0:T(4,128)S(1)} copy(f32[8,3,6]{0,1,2:T(4,128)} %bitcast.19) | data formatting | bytes 1152 | tf_op jit(solution)/shard_map/transpose | solution.py:341
  5.4 0.7 %reshape.18.cyc_b = f32[8,18]{1,0:T(8,128)} reshape(f32[8,3,6]{2,1,0:T(4,128)S(1)} %copy.21) | data formatting | bytes 1152 | tf_op jit(solution)/shard_map/reshape | solution.py:341
  6.0 0.8 %convert_bitcast_fusion = f32[5,8,3,64]{3,1,2,0:T(8,128)S(1)} fusion(bf16[64,8,5,3]{0,1,3,2:T(8,128)(2,1)} %param.11), kind=kLoop, calls=%fused_computation.5 | loop fusion | flops 7680 | bytes 46080 | tf_op jit(solution)/shard_map/convert_element_type | solution.py:333
  6.8 0.1 reshape.19
  6.9 0.7 %select_maximum_fusion.taps = f32[48,384]{1,0:T(8,128)} fusion(f32[40,192]{1,0:T(8,128)S(1)} %reshape.19), kind=kLoop, calls=%fused_computation.2 | loop fusion | flops 92160 | bytes 104448 | tf_op jit(solution)/shard_map/concatenate | solution.py:334
  7.7 4.0 %copy_bitcast_fusion = (bf16[16,64,512]{2,1,0:T(8,128)(2,1)}, bf16[16,64,512]{2,1,0:T(8,128)(2,1)}) fusion(bf16[64,16,512]{2,1,0:T(8,128)(2,1)} %param.8, bf16[64,16,512]{2,1,0:T(8,128)(2,1)} %param.7), kind=kLoop, calls=%fused_computation | loop fusion | bytes 4194304 | tf_op jit(solution)/shard_map/transpose | solution.py:331
  11.7 45.6 %shard_map.94 = (bf16[16,64,512]{2,1,0:T(8,128)(2,1)}, bf16[16,64,512]{2,1,0:T(8,128)(2,1)}, f32[3,32,512]{2,1,0:T(8,128)}) custom-call(bf16[16,64,512]{2,1,0:T(8,128)(2,1)} %get-tuple-element.16.field, bf16[16,64,512]{2,1,0:T(8,128)(2,1)} %get-tuple-element.15.cot_hbm, bf16[3,512,512]{2,1,0:T(8,128)(2,1)} %bitcast.13, f32[48,384]{1,0:T(8,128)} %select_maximum_fusion.taps, ...), custom_call_target="tpu_custom_call" | custom-call | tf_op jit(solution)/shard_map/pallas_call | solution.py:349
  57.3 0.0 copy-start
  57.3 2.9 %copy.22 = bf16[64,16,512]{2,1,0:T(8,128)(2,1)} copy(bf16[64,16,512]{2,0,1:T(8,128)(2,1)} %bitcast.15) | data formatting | bytes 2097152
  60.1 0.0 copy-start.1
  60.1 0.0 copy-done
  60.1 1.5 %copy.23 = bf16[64,16,512]{2,1,0:T(8,128)(2,1)} copy(bf16[64,16,512]{2,0,1:T(8,128)(2,1)S(1)} %bitcast.14) | data formatting | bytes 2097152
  61.7 0.0 copy-done.1
  61.7 0.7 %copy.28 = f32[32,3,512]{2,0,1:T(8,128)} copy(f32[32,3,512]{2,0,1:T(8,128)S(1)} %bitcast.16) | data formatting | bytes 393216
  (1 shorter events, 0.0 us)
Async XLA Ops:
  57.3 2.9 %copy-start = (bf16[16,64,512]{2,1,0:T(8,128)(2,1)S(1)}, bf16[16,64,512]{2,1,0:T(8,128)(2,1)}, u32[]{:S(2)}) copy-start(bf16[16,64,512]{2,1,0:T(8,128)(2,1)} %get-tuple-element.7) | copy-start | bytes 3145732
  60.1 1.6 %copy-start.1 = (f32[3,32,512]{2,1,0:T(8,128)S(1)}, f32[3,32,512]{2,1,0:T(8,128)}, u32[]{:S(2)}) copy-start(f32[3,32,512]{2,1,0:T(8,128)} %get-tuple-element.8) | copy-start | bytes 589828
where the time goes:
time: 62.8 us; the launch traced here: 62.4 us
  Pallas kernels  45.6 us (73%)
  local copies, waits for them, and re-layouts  14.7 us (23%)
  other arithmetic  1.47 us (2%)
  between operations  0.66 us (1%)
    pallas_call x1, Pallas kernels, body(): pl.pallas_call(functools.partial(kernel_body, n, direct, scale), out_shap...  45.6 us
    unnamed x8, local copies, waits for them, and re-layouts  5.8 us
    transpose x1, local copies, waits for them, and re-layouts, body(): cot_t = jnp.swapaxes(cotangent, 0, 1)  4.01 us
    another operation x2, local copies, waits for them, and re-layouts, body(): wids = jnp.tile(widths, 2 * K)[None]  1.31 us
    another operation x2, local copies, waits for them, and re-layouts, body(): offs = jnp.tile(offsets, 2 * K)[None]  1.31 us

commit v1 on v0

--- a/solution.py
+++ b/solution.py
@@ -28,8 +28,7 @@
     taps,
     offs,
     wids,
-    cyc_f,
-    cyc_b,
+    cyc,
     out,
     fgrad,
     mgrad,
@@ -49,6 +48,8 @@
     part,
     partb,
     r1,
+    s1,
+    ry,
     s2,
     r2,
     in_sem,
@@ -62,6 +63,8 @@
     s_recv,
     a_send,
     a_recv,
+    c_send,
+    c_recv,
     b_send,
     b_recv,
 ):
@@ -87,6 +90,13 @@
     load_field.start()
     load_mix.start()
     load_cot.start()
+
+    def loop(lo, hi, fn):
+        def step(i, carry):
+            fn(i)
+            return carry
+
+        lax.fori_loop(lo, hi, step, 0)
 
     def remote(src, dst, send, recv, peer):
         return pltpu.make_async_remote_copy(
@@ -98,25 +108,36 @@
             device_id_type=MESH,
         )
 
-    def spread(buf, send, recv):
+    quads = n // 4
+    quad = me // 4
+    spot = lax.rem(me, 4)
+
+    def near(buf, send, recv):
         def copy(d):
-            return remote(buf.at[0], buf.at[d], send.at[d], recv.at[d], lax.rem(me + d, n))
+            peer = quad * 4 + lax.rem(spot + d, 4)
+            return remote(buf.at[0], buf.at[d], send.at[d], recv.at[d], peer)
 
         return copy
 
-    def start_all(copy):
-        def step(d, carry):
-            copy(d).start()
-            return carry
-
-        lax.fori_loop(1, n, step, 0)
-
-    def wait_all(copy):
-        def step(d, carry):
-            copy(d).wait()
-            return carry
-
-        lax.fori_loop(1, n, step, 0)
+    def far(buf, send, recv):
+        def copy(d):
+            peer = lax.rem(quad + d, quads) * 4 + spot
+            return remote(
+                buf.at[4], buf.at[4 + d], send.at[4 + d], recv.at[4 + d], peer
+            )
+
+        return copy
+
+    def start_all(copy, count):
+        loop(1, count, lambda d: copy(d).start())
+
+    def wait_all(copy, count):
+        loop(1, count, lambda d: copy(d).wait())
+
+    def turn(buf, send, recv):
+        wait_all(near(buf, send, recv), 4)
+        buf[4] = jnp.sum(buf[0:4], axis=0)
+        start_all(far(buf, send, recv), quads)
 
     pl.semaphore_wait(barrier, n - 1)
     halo_l = remote(
@@ -129,17 +150,21 @@
     halo_r.start()
     load_field.wait()
     zbuf[0] = jnp.sum(xt[R : R + cols, 0:16, :].astype(F32), axis=0)[0:PB]
-    zonal_copy = spread(zbuf, z_send, z_recv)
-    start_all(zonal_copy)
+    start_all(near(zbuf, z_send, z_recv), 4)
 
     wide = 2 * K * lat
-    rel = lax.broadcasted_iota(jnp.int32, (lat, wide), 0) - offs[...]
-    used = rel < wids[...]
+    rel = lax.broadcasted_iota(jnp.int32, (lat, wide), 0) - jnp.concatenate(
+        [offs[...]] * (2 * K), axis=1
+    )
+    used = rel < jnp.concatenate([wids[...]] * (2 * K), axis=1)
+    blank = jnp.zeros((BAND, lat), F32)
     for t in range(TAPS + 1):
+        first = [taps[t, k].astype(F32) if t < TAPS else blank for k in range(K)]
+        second = [taps[t - 1, k].astype(F32) if t > 0 else blank for k in range(K)]
+        rows_bk = jnp.concatenate(first + second, axis=1)
         acc = jnp.zeros((lat, wide), F32)
         for b in range(BAND):
-            row = taps[t * BAND + b : t * BAND + b + 1, :]
-            acc = jnp.where((rel == b) & used, row, acc)
+            acc = jnp.where((rel == b) & used, rows_bk[b : b + 1, :], acc)
         pieces[t * lat : (t + 1) * lat, :] = acc
     fwd[...] = pieces[...].T.astype(BF16)
     for a in range(4):
@@ -151,6 +176,8 @@
                 block = jnp.zeros((lat, wide), BF16)
             bwd[a * lat : (a + 1) * lat, p * wide : (p + 1) * wide] = block
 
+    turn(zbuf, z_send, z_recv)
+
     def conv_pair(p):
         source = xt[pl.ds(2 * p, TAPS + 1)].reshape((TAPS + 1) * lat, ch)
         c = jnp.dot(fwd[...], source, preferred_element_type=F32)
@@ -158,25 +185,23 @@
         polar[pl.ds(2 * p, 2)] = c[:, :, 0:16]
         conv[pl.ds(2 * p, 2)] = c.astype(BF16)
 
-    def loop(lo, hi, fn):
-        def step(i, carry):
-            fn(i)
-            return carry
-
-        lax.fori_loop(lo, hi, step, 0)
-
     pairs = cols // 2
     loop(1, pairs - 1, conv_pair)
     halo_l.wait()
     halo_r.wait()
     loop(0, 2, lambda i: conv_pair(i * (pairs - 1)))
 
-    wait_all(zonal_copy)
-    zonal = jnp.sum(zbuf[...], axis=0) * scale
-    term = jnp.zeros((K * 16, ch), F32)
-    for p in range(PB):
-        term = term + cyc_f[:, p : p + 1] * zonal[p : p + 1, :]
-    term = term.reshape(1, K, 16, ch)
+    wait_all(far(zbuf, z_send, z_recv), quads)
+    zonal = jnp.sum(zbuf[4:], axis=0) * scale
+    lines = []
+    for k in range(K):
+        for i in range(POLAR):
+            line = cyc[i, k, 0] * zonal[0:1]
+            for p in range(1, PB):
+                line = line + cyc[i, k, p] * zonal[p : p + 1]
+            lines.append(line)
+        lines.append(jnp.zeros((16 - POLAR, ch), F32))
+    term = jnp.concatenate(lines, axis=0).reshape(1, K, 16, ch)
     load_mix.wait()
     load_cot.wait()
     ms[...] = jnp.zeros_like(ms)
@@ -210,41 +235,68 @@
     grad_r.start()
     loop(1, groups - 1, mix_group)
     sbuf[0] = ms[0:PB]
-    sums_copy = spread(sbuf, s_send, s_recv)
-    start_all(sums_copy)
+    start_all(near(sbuf, s_send, s_recv), 4)
 
     half = ch // 2
     if direct:
         rows = ch // n
-        chips = n // 2
         core = lax.rem(me, 2)
-        chip = me // 2
-        sibling = chip * 2 + (1 - core)
-        per = half // (2 * rows)
-
-        def pair_copy(k):
+        side = lax.rem(me // 2, 2)
+        per = half // (4 * rows)
+
+        def core_copy(k):
             return remote(
-                partb.at[k, 1 - core], r1.at[k], a_send.at[k], a_recv.at[k], sibling
-            )
-
-        def chip_copy(k, d):
+                partb.at[k, 1 - core],
+                r1.at[k],
+                a_send.at[k],
+                a_recv.at[k],
+                quad * 4 + side * 2 + (1 - core),
+            )
+
+        def side_copy(k):
+            return remote(
+                s1.at[k],
+                ry.at[k],
+                c_send.at[k],
+                c_recv.at[k],
+                quad * 4 + (1 - side) * 2 + core,
+            )
+
+        def quad_copy(k, d):
             return remote(
                 s2.at[k, d],
                 r2.at[k, d],
                 b_send.at[k, d],
                 b_recv.at[k, d],
-                lax.rem(chip + d, chips) * 2 + core,
-            )
-
-        def pass_on(k):
-            pair_copy(k).wait()
+                lax.rem(quad + d, quads) * 4 + spot,
+            )
+
+        def pass_side(k):
+            core_copy(k).wait()
+
+            def step(z):
+                s1[k, z] = (
+                    part[k, core, 1 - side, z] + r1[k, 1 - side, z].astype(F32)
+                ).astype(BF16)
+
+            loop(0, quads, step)
+            side_copy(k).start()
+
+        def own(k, z):
+            return (
+                part[k, core, side, z]
+                + r1[k, side, z].astype(F32)
+                + ry[k, z].astype(F32)
+            )
+
+        def pass_quads(k):
+            side_copy(k).wait()
 
             def step(d):
-                to = lax.rem(chip + d, chips)
-                s2[k, d] = (part[k, core, to] + r1[k, to].astype(F32)).astype(BF16)
-                chip_copy(k, d).start()
-
-            loop(1, chips, step)
+                s2[k, d] = own(k, lax.rem(quad + d, quads)).astype(BF16)
+                quad_copy(k, d).start()
+
+            loop(1, quads, step)
 
     for k in range(K):
 
@@ -259,19 +311,23 @@
             if not direct:
                 mgrad[k, lanes, :] = res
                 return
-            res = res.reshape(per, 2, rows, ch)
+            res = res.reshape(per, 2, 2, rows, ch)
             resb = res.astype(BF16)
-            for c in range(2):
-                part[k, c, pl.ds(h * per, per)] = res[:, c]
-                partb[k, c, pl.ds(h * per, per)] = resb[:, c]
+            for y in range(2):
+                for c in range(2):
+                    part[k, c, y, pl.ds(h * per, per)] = res[:, y, c]
+                    partb[k, c, y, pl.ds(h * per, per)] = resb[:, y, c]
 
         loop(0, 2, product)
         if direct:
-            pair_copy(k).start()
+            core_copy(k).start()
             if k > 0:
-                pass_on(k - 1)
+                pass_side(k - 1)
+        if k == 0:
+            turn(sbuf, s_send, s_recv)
     if direct:
-        pass_on(K - 1)
+        pass_quads(0)
+        pass_side(K - 1)
 
     def spread_grad(g):
         at = pl.ds(4 * g, 4)
@@ -286,23 +342,25 @@
     grad_l.wait()
     grad_r.wait()
     loop(0, 2, lambda i: spread_grad(i * groups))
-
-    wait_all(sums_copy)
-    total = jnp.sum(sbuf[...], axis=0)
+    if direct:
+        pass_quads(1)
+
+    wait_all(far(sbuf, s_send, s_recv), quads)
+    total = jnp.sum(sbuf[4:], axis=0)
     high = total.astype(BF16)
     low = (total - high.astype(F32)).astype(BF16)
     both = jnp.concatenate([high.astype(F32), low.astype(F32)], axis=0).astype(BF16)
-    zgrad = jnp.zeros((PB, ch), F32)
+    lines = [jnp.zeros((1, ch), F32)] * PB
     for k in range(K):
         res = lax.dot_general(
             both, mix[k], (((1,), (1,)), ((), ())), preferred_element_type=F32
         )
         res = res[0:PB] + res[PB : 2 * PB]
         for i in range(POLAR):
-            at = k * POLAR + i
-            zgrad = zgrad + cyc_b[:, at : at + 1] * res[i : i + 1, :]
-    zgrad = zgrad * scale
-    zgrad = jnp.concatenate([zgrad, jnp.zeros((16 - PB, ch), F32)], axis=0)[None]
+            for q in range(PB):
+                lines[q] = lines[q] + (cyc[i, k, q] * scale) * res[i : i + 1]
+    lines.append(jnp.zeros((16 - PB, ch), F32))
+    zgrad = jnp.concatenate(lines, axis=0)[None]
 
     def field_group(g):
         at = pl.ds(4 * g, 4)
@@ -314,10 +372,11 @@
     loop(0, groups, field_group)
 
     if direct:
+        pass_quads(K - 1)
         for k in range(K):
-            acc = part[k, core, chip] + r1[k, chip].astype(F32)
-            for d in range(1, chips):
-                chip_copy(k, d).wait()
+            acc = own(k, quad)
+            for d in range(1, quads):
+                quad_copy(k, d).wait()
                 acc = acc + r2[k, d].astype(F32)
             mgrad[k] = acc
 
@@ -326,23 +385,18 @@
     lat, cols, ch = field.shape
     scale = float(cols * n) ** (-0.5)
     rows = ch // n
-    direct = n % 2 == 0 and n > 2 and rows % 16 == 0
+    direct = rows % 16 == 0 and ch % (8 * rows) == 0
     field_t = jnp.swapaxes(field, 0, 1)
     cot_t = jnp.swapaxes(cotangent, 0, 1)
     mix_t = jnp.swapaxes(mixing, 0, 1)
-    taps = jnp.transpose(kernel, (2, 1, 3, 0)).reshape(TAPS * BAND, K * lat).astype(F32)
-    taps = jnp.concatenate(
-        [jnp.pad(taps, ((0, BAND), (0, 0))), jnp.pad(taps, ((BAND, 0), (0, 0)))], axis=1
-    )
-    offs = jnp.tile(offsets, 2 * K)[None]
-    wids = jnp.tile(widths, 2 * K)[None]
-    cyc_f = jnp.pad(jnp.transpose(cycle, (2, 0, 1)), ((0, 0), (0, 16 - POLAR), (0, 0)))
-    cyc_f = cyc_f.reshape(K * 16, PB)
-    cyc_b = jnp.transpose(cycle, (1, 2, 0)).reshape(PB, K * POLAR)
+    taps = jnp.transpose(kernel, (2, 3, 1, 0))
+    offs = offsets.reshape(1, lat)
+    wids = widths.reshape(1, lat)
+    cyc = jnp.swapaxes(cycle, 1, 2)
 
     wide = 2 * K * lat
     dma = pltpu.SemaphoreType.DMA
-    chips = n // 2 if direct else 1
+    quads = n // 4 if direct else 1
     brows = rows if direct else 16
     vmem = pl.BlockSpec(memory_space=pltpu.VMEM)
     hbm = pl.BlockSpec(memory_space=pl.ANY)
@@ -353,7 +407,7 @@
             jax.ShapeDtypeStruct((cols, lat, ch), BF16),
             jax.ShapeDtypeStruct((K, rows if direct else ch, ch), F32),
         ],
-        in_specs=[hbm] * 3 + [vmem] * 5,
+        in_specs=[hbm] * 3 + [vmem] * 3 + [pl.BlockSpec(memory_space=pltpu.SMEM)],
         out_specs=[vmem] * 3,
         scratch_shapes=[
             pltpu.VMEM((cols + 2 * R, lat, ch), BF16),
@@ -367,31 +421,35 @@
             pltpu.VMEM((cols + 2 * R, lat, ch), BF16),
             pltpu.VMEM((cols + 2 * R, K, lat, ch), BF16),
             pltpu.VMEM((16, ch), F32),
-            pltpu.VMEM((n, PB, ch), F32),
-            pltpu.VMEM((n, PB, ch), F32),
-            pltpu.VMEM((K, 2, chips, brows, ch), F32),
-            pltpu.VMEM((K, 2, chips, brows, ch), BF16),
-            pltpu.VMEM((K, chips, brows, ch), BF16),
-            pltpu.VMEM((K, chips, brows, ch), BF16),
-            pltpu.VMEM((K, chips, brows, ch), BF16),
+            pltpu.VMEM((4 + n // 4, PB, ch), F32),
+            pltpu.VMEM((4 + n // 4, PB, ch), F32),
+            pltpu.VMEM((K, 2, 2, quads, brows, ch), F32),
+            pltpu.VMEM((K, 2, 2, quads, brows, ch), BF16),
+            pltpu.VMEM((K, 2, quads, brows, ch), BF16),
+            pltpu.VMEM((K, quads, brows, ch), BF16),
+            pltpu.VMEM((K, quads, brows, ch), BF16),
+            pltpu.VMEM((K, quads, brows, ch), BF16),
+            pltpu.VMEM((K, quads, brows, ch), BF16),
             dma((3,)),
             dma((2,)),
             dma((2,)),
             dma((2,)),
             dma((2,)),
-            dma((n,)),
-            dma((n,)),
-            dma((n,)),
-            dma((n,)),
+            dma((4 + n // 4,)),
+            dma((4 + n // 4,)),
+            dma((4 + n // 4,)),
+            dma((4 + n // 4,)),
             dma((K,)),
             dma((K,)),
-            dma((K, chips)),
-            dma((K, chips)),
+            dma((K,)),
+            dma((K,)),
+            dma((K, quads)),
+            dma((K, quads)),
         ],
         compiler_params=pltpu.CompilerParams(
             collective_id=0, has_side_effects=True, vmem_limit_bytes=56 * 1024 * 1024
         ),
-    )(field_t, cot_t, mix_t, taps, offs, wids, cyc_f, cyc_b)
+    )(field_t, cot_t, mix_t, taps, offs, wids, cyc)
     output = jnp.swapaxes(out_t, 0, 1)
     field_grad = jnp.swapaxes(fgrad_t, 0, 1)
     mixing_grad = jnp.swapaxes(mgrad_t, 0, 1)

time: 62.8 us -> 50.9 us (0.81)
  local copies, waits for them, and re-layouts: 14.7 us -> 9.11 us
  Pallas kernels: 45.6 us -> 40.9 us
  other arithmetic: 1.47 us -> 0 us
    pallas_call x1, Pallas kernels: 45.6 us -> 40.9 us  [body(): pl.pallas_call(functools.partial(kernel_body, n, direct, scale), out_shap...]
    another operation x4 -> x0, local copies, waits for them, and re-layouts: 2.62 us -> none  [the longest x2 1.31 us: body(): wids = jnp.tile(widths, 2 * K)[None]]
    transpose x1 -> x0, local copies, waits for them, and re-layouts: 0.8 us -> none  [body(): cyc_b = jnp.transpose(cycle, (1, 2, 0)).reshape(PB, K * POLAR)]
    convert_element_type x1 -> x0, other arithmetic: 0.76 us -> none  [body(): jnp.transpose(kernel, (2, 1, 3, 0)).reshape(TAPS * BAND, K * lat)]
    concatenate x1 -> x0, other arithmetic: 0.71 us -> none  [body(): jnp.concatenate([jnp.pad(taps, ((0, BAND), (0, 0))), jnp.pad(taps, ((BAND...]
    unnamed x8 -> x7, local copies, waits for them, and re-layouts: 5.8 us -> 5.09 us
    reshape x1 -> x0, local copies, waits for them, and re-layouts: 0.67 us -> none  [body(): cyc_b = jnp.transpose(cycle, (1, 2, 0)).reshape(PB, K * POLAR)]
where the time goes in v1:
time: 50.9 us; the launch traced here: 50.7 us
  Pallas kernels  40.9 us (80%)
  local copies, waits for them, and re-layouts  9.11 us (18%)
  between operations  0.65 us (1%)
    pallas_call x1, Pallas kernels, body(): pl.pallas_call(functools.partial(kernel_body, n, direct, scale), out_shap...  40.9 us
    unnamed x7, local copies, waits for them, and re-layouts  5.09 us
    transpose x1, local copies, waits for them, and re-layouts, body(): cot_t = jnp.swapaxes(cotangent, 0, 1)  4.02 us

profile of v1, /device:TPU:0, one launch (start us, length us, event | category | flops | bytes accessed | tf_op | source)
XLA Modules:
  0.0 50.7 jit_solution(666979862996400951)
XLA Ops:
  0.6 4.0 %copy_bitcast_fusion = (bf16[16,64,512]{2,1,0:T(8,128)(2,1)}, bf16[16,64,512]{2,1,0:T(8,128)(2,1)}) fusion(bf16[64,16,512]{2,1,0:T(8,128)(2,1)} %param.8, bf16[64,16,512]{2,1,0:T(8,128)(2,1)} %param.7), kind=kLoop, calls=%fused_computation | loop fusion | bytes 4194304 | tf_op jit(solution)/shard_map/transpose | solution.py:390
  4.6 40.9 %shard_map.94 = (bf16[16,64,512]{2,1,0:T(8,128)(2,1)}, bf16[16,64,512]{2,1,0:T(8,128)(2,1)}, f32[3,32,512]{2,1,0:T(8,128)}) custom-call(bf16[16,64,512]{2,1,0:T(8,128)(2,1)} %get-tuple-element.13.field, bf16[16,64,512]{2,1,0:T(8,128)(2,1)} %get-tuple-element.12.cot_hbm, bf16[3,512,512]{2,1,0:T(8,128)(2,1)} %bitcast.12, bf16[5,3,8,64]{3,2,1,0:T(8,128)(2,1)} %bitcast.16, ...), custom_call_target="tpu_custom_call" | custom-call | tf_op jit(solution)/shard_map/pallas_call | solution.py:403
  45.6 0.0 copy-start
  45.6 2.9 %copy.12 = bf16[64,16,512]{2,1,0:T(8,128)(2,1)} copy(bf16[64,16,512]{2,0,1:T(8,128)(2,1)} %bitcast.14) | data formatting | bytes 2097152
  48.4 0.0 copy-start.1
  48.4 0.0 copy-done
  48.5 1.5 %copy.13 = bf16[64,16,512]{2,1,0:T(8,128)(2,1)} copy(bf16[64,16,512]{2,0,1:T(8,128)(2,1)S(1)} %bitcast.13) | data formatting | bytes 2097152
  50.0 0.0 copy-done.1
  50.0 0.7 %copy.17 = f32[32,3,512]{2,0,1:T(8,128)} copy(f32[32,3,512]{2,0,1:T(8,128)S(1)} %bitcast.15) | data formatting | bytes 393216
Async XLA Ops:
  45.6 2.9 %copy-start = (bf16[16,64,512]{2,1,0:T(8,128)(2,1)S(1)}, bf16[16,64,512]{2,1,0:T(8,128)(2,1)}, u32[]{:S(2)}) copy-start(bf16[16,64,512]{2,1,0:T(8,128)(2,1)} %get-tuple-element.7) | copy-start | bytes 3145732
  48.4 1.6 %copy-start.1 = (f32[3,32,512]{2,1,0:T(8,128)S(1)}, f32[3,32,512]{2,1,0:T(8,128)}, u32[]{:S(2)}) copy-start(f32[3,32,512]{2,1,0:T(8,128)} %get-tuple-element.8) | copy-start | bytes 589828

commit v2 on v1

--- a/solution.py
+++ b/solution.py
@@ -447,7 +447,7 @@
             dma((K, quads)),
         ],
         compiler_params=pltpu.CompilerParams(
-            collective_id=0, has_side_effects=True, vmem_limit_bytes=56 * 1024 * 1024
+            collective_id=0, has_side_effects=True, vmem_limit_bytes=36 * 1024 * 1024
         ),
     )(field_t, cot_t, mix_t, taps, offs, wids, cyc)
     output = jnp.swapaxes(out_t, 0, 1)

time: 50.9 us -> 46.4 us (0.912)
  local copies, waits for them, and re-layouts: 9.11 us -> 6.61 us
  Pallas kernels: 40.9 us -> 38.9 us
    pallas_call x1, Pallas kernels: 40.9 us -> 38.9 us  [body(): pl.pallas_call(functools.partial(kernel_body, n, direct, scale), out_shap...]
    unnamed x7 -> x13, local copies, waits for them, and re-layouts: 5.09 us -> 3.79 us
    transpose x1, local copies, waits for them, and re-layouts: 4.02 us -> 2.81 us  [body(): cot_t = jnp.swapaxes(cotangent, 0, 1)]
where the time goes in v2:
time: 46.4 us; the launch traced here: 46.3 us
  Pallas kernels  38.9 us (84%)
  local copies, waits for them, and re-layouts  6.61 us (14%)
  between operations  0.72 us (2%)
    pallas_call x1, Pallas kernels, body(): pl.pallas_call(functools.partial(kernel_body, n, direct, scale), out_shap...  38.9 us
    unnamed x13, local copies, waits for them, and re-layouts  3.79 us
    transpose x1, local copies, waits for them, and re-layouts, body(): cot_t = jnp.swapaxes(cotangent, 0, 1)  2.81 us

profile of v2, /device:TPU:0, one launch (start us, length us, event | category | flops | bytes accessed | tf_op | source)
XLA Modules:
  0.0 46.3 jit_solution(9926724701021299579)
XLA Ops:
  0.6 0.0 copy-start
  0.6 0.0 copy-start.1
  0.7 0.0 copy-start.2
  0.7 0.0 copy-start.3
  0.7 0.0 copy-start.4
  0.7 2.8 %copy_bitcast_fusion = (bf16[16,64,512]{2,1,0:T(8,128)(2,1)S(1)}, bf16[16,64,512]{2,1,0:T(8,128)(2,1)S(1)}) fusion(bf16[64,16,512]{2,1,0:T(8,128)(2,1)} %param.8, bf16[64,16,512]{2,1,0:T(8,128)(2,1)} %param.7), kind=kLoop, calls=%fused_computation | loop fusion | bytes 4194304 | tf_op jit(solution)/shard_map/transpose | solution.py:390
  3.5 0.0 copy-done
  3.5 0.0 copy-done.1
  3.5 0.0 copy-done.2
  3.5 0.0 copy-done.3
  3.5 0.0 copy-done.4
  3.5 38.9 %shard_map.94 = (bf16[16,64,512]{2,1,0:T(8,128)(2,1)S(1)}, bf16[16,64,512]{2,1,0:T(8,128)(2,1)S(1)}, f32[3,32,512]{2,1,0:T(8,128)S(1)}) custom-call(bf16[16,64,512]{2,1,0:T(8,128)(2,1)S(1)} %get-tuple-element.13.field, bf16[16,64,512]{2,1,0:T(8,128)(2,1)S(1)} %get-tuple-element.12.cot_hbm, bf16[3,512,512]{2,1,0:T(8,128)(2,1)S(1)} %bitcast.12, ...), custom_call_target="tpu_custom_call" | custom-call | tf_op jit(solution)/shard_map/pallas_call | solution.py:403
  42.5 1.5 %copy.12 = bf16[64,16,512]{2,1,0:T(8,128)(2,1)} copy(bf16[64,16,512]{2,0,1:T(8,128)(2,1)S(1)} %bitcast.14) | data formatting | bytes 2097152
  44.0 1.5 %copy.13 = bf16[64,16,512]{2,1,0:T(8,128)(2,1)} copy(bf16[64,16,512]{2,0,1:T(8,128)(2,1)S(1)} %bitcast.13) | data formatting | bytes 2097152
  45.6 0.7 %copy.17 = f32[32,3,512]{2,0,1:T(8,128)} copy(f32[32,3,512]{2,0,1:T(8,128)S(1)} %bitcast.15) | data formatting | bytes 393216
Async XLA Ops:
  0.6 2.9 %copy-start = (bf16[512,3,512]{2,0,1:T(8,128)(2,1)S(1)}, bf16[512,3,512]{2,0,1:T(8,128)(2,1)}, u32[]{:S(2)}) copy-start(bf16[512,3,512]{2,0,1:T(8,128)(2,1)} %param.13) | copy-start | bytes 4718596
  0.6 2.9 %copy-start.1 = (bf16[64,8,5,3]{0,1,3,2:T(8,128)(2,1)S(1)}, bf16[64,8,5,3]{0,1,3,2:T(8,128)(2,1)}, u32[]{:S(2)}) copy-start(bf16[64,8,5,3]{0,1,3,2:T(8,128)(2,1)} %param.11) | copy-start | bytes 46084
  0.7 2.9 %copy-start.2 = (f32[6,8,3]{1,2,0:T(4,128)S(1)}, f32[6,8,3]{1,2,0:T(4,128)}, u32[]{:S(2)}) copy-start(f32[6,8,3]{1,2,0:T(4,128)} %param.12) | copy-start | bytes 1732
  0.7 2.9 %copy-start.3 = (s32[64]{0:T(128)S(1)}, s32[64]{0:T(128)}, u32[]{:S(2)}) copy-start(s32[64]{0:T(128)} %param.9) | copy-start | bytes 772
  0.7 2.9 %copy-start.4 = (s32[64]{0:T(128)S(1)}, s32[64]{0:T(128)}, u32[]{:S(2)}) copy-start(s32[64]{0:T(128)} %param.10) | copy-start | bytes 772

commit v3 on v2

--- a/solution.py
+++ b/solution.py
@@ -191,6 +191,32 @@
     halo_r.wait()
     loop(0, 2, lambda i: conv_pair(i * (pairs - 1)))
 
+    load_mix.wait()
+    load_cot.wait()
+
+    def mix_rows(first, count, lo, hi):
+        at = pl.ds(first, count)
+        size, shape = count * (hi - lo), (count, hi - lo, ch)
+        mixed = jnp.dot(
+            conv[at, 0, lo:hi].reshape(size, ch), mix[0], preferred_element_type=F32
+        )
+        for k in range(1, K):
+            mixed = mixed + jnp.dot(
+                conv[at, k, lo:hi].reshape(size, ch), mix[k], preferred_element_type=F32
+            )
+        sig = jax.nn.sigmoid(mixed)
+        out[at, lo:hi] = (mixed * sig).astype(BF16).reshape(shape)
+        ct = cot[at, lo:hi].reshape(size, ch).astype(F32)
+        grad = (ct * (sig * (1.0 + mixed * (1.0 - sig)))).astype(BF16).reshape(shape)
+        mg[pl.ds(R + first, count), lo:hi] = grad
+        return grad
+
+    groups = cols // 4
+
+    def mix_group(g):
+        mix_rows(4 * g, 4, 16, lat)
+
+    loop(0, groups, mix_group)
     wait_all(far(zbuf, z_send, z_recv), quads)
     zonal = jnp.sum(zbuf[4:], axis=0) * scale
     lines = []
@@ -202,29 +228,8 @@
             lines.append(line)
         lines.append(jnp.zeros((16 - POLAR, ch), F32))
     term = jnp.concatenate(lines, axis=0).reshape(1, K, 16, ch)
-    load_mix.wait()
-    load_cot.wait()
-    ms[...] = jnp.zeros_like(ms)
-
-    def mix_group(g):
-        at = pl.ds(4 * g, 4)
-        conv[at, :, 0:16] = (polar[at] + term).astype(BF16)
-        mixed = jnp.dot(
-            conv[at, 0].reshape(4 * lat, ch), mix[0], preferred_element_type=F32
-        )
-        for k in range(1, K):
-            mixed = mixed + jnp.dot(
-                conv[at, k].reshape(4 * lat, ch), mix[k], preferred_element_type=F32
-            )
-        sig = jax.nn.sigmoid(mixed)
-        out[at] = (mixed * sig).astype(BF16).reshape(4, lat, ch)
-        ct = cot[at].reshape(4 * lat, ch).astype(F32)
-        grad = (ct * (sig * (1.0 + mixed * (1.0 - sig)))).astype(BF16).reshape(4, lat, ch)
-        mg[pl.ds(R + 4 * g, 4)] = grad
-        ms[...] += jnp.sum(grad[:, 0:16].astype(F32), axis=0)
-
-    groups = cols // 4
-    loop(0, 2, lambda i: mix_group(i * (groups - 1)))
+    conv[:, :, 0:16] = (polar[...] + term).astype(BF16)
+    ms[...] = jnp.sum(mix_rows(0, cols, 0, 16).astype(F32), axis=0)
     grad_l = remote(
         mg.at[pl.ds(R, R)], mg.at[pl.ds(R + cols, R)], g_send.at[0], g_recv.at[0], left
     )
@@ -233,7 +238,6 @@
     )
     grad_l.start()
     grad_r.start()
-    loop(1, groups - 1, mix_group)
     sbuf[0] = ms[0:PB]
     start_all(near(sbuf, s_send, s_recv), 4)
 

time: 46.4 us -> 46.9 us (1.011)
  Pallas kernels: 38.9 us -> 39.5 us
    pallas_call x1, Pallas kernels: 38.9 us -> 39.5 us  [body(): pl.pallas_call(functools.partial(kernel_body, n, direct, scale), out_shap...]
where the time goes in v3:
time: 46.9 us; the launch traced here: 46.8 us
  Pallas kernels  39.5 us (84%)
  local copies, waits for them, and re-layouts  6.61 us (14%)
  between operations  0.72 us (2%)
    pallas_call x1, Pallas kernels, body(): pl.pallas_call(functools.partial(kernel_body, n, direct, scale), out_shap...  39.5 us
    unnamed x13, local copies, waits for them, and re-layouts  3.79 us
    transpose x1, local copies, waits for them, and re-layouts, body(): cot_t = jnp.swapaxes(cotangent, 0, 1)  2.81 us

profile of v3, /device:TPU:0, one launch (start us, length us, event | category | flops | bytes accessed | tf_op | source)
XLA Modules:
  0.0 46.8 jit_solution(7514959585469374315)
XLA Ops:
  0.6 0.0 copy-start
  0.6 0.0 copy-start.1
  0.7 0.0 copy-start.2
  0.7 0.0 copy-start.3
  0.7 0.0 copy-start.4
  0.7 2.8 %copy_bitcast_fusion = (bf16[16,64,512]{2,1,0:T(8,128)(2,1)S(1)}, bf16[16,64,512]{2,1,0:T(8,128)(2,1)S(1)}) fusion(bf16[64,16,512]{2,1,0:T(8,128)(2,1)} %param.8, bf16[64,16,512]{2,1,0:T(8,128)(2,1)} %param.7), kind=kLoop, calls=%fused_computation | loop fusion | bytes 4194304 | tf_op jit(solution)/shard_map/transpose | solution.py:394
  3.5 0.0 copy-done
  3.5 0.0 copy-done.1
  3.5 0.0 copy-done.2
  3.5 0.0 copy-done.3
  3.5 0.0 copy-done.4
  3.5 39.5 %shard_map.94 = (bf16[16,64,512]{2,1,0:T(8,128)(2,1)S(1)}, bf16[16,64,512]{2,1,0:T(8,128)(2,1)S(1)}, f32[3,32,512]{2,1,0:T(8,128)S(1)}) custom-call(bf16[16,64,512]{2,1,0:T(8,128)(2,1)S(1)} %get-tuple-element.13.field, bf16[16,64,512]{2,1,0:T(8,128)(2,1)S(1)} %get-tuple-element.12.cot_hbm, bf16[3,512,512]{2,1,0:T(8,128)(2,1)S(1)} %bitcast.12, ...), custom_call_target="tpu_custom_call" | custom-call | tf_op jit(solution)/shard_map/pallas_call | solution.py:407
  43.0 1.5 %copy.12 = bf16[64,16,512]{2,1,0:T(8,128)(2,1)} copy(bf16[64,16,512]{2,0,1:T(8,128)(2,1)S(1)} %bitcast.14) | data formatting | bytes 2097152
  44.6 1.5 %copy.13 = bf16[64,16,512]{2,1,0:T(8,128)(2,1)} copy(bf16[64,16,512]{2,0,1:T(8,128)(2,1)S(1)} %bitcast.13) | data formatting | bytes 2097152
  46.1 0.7 %copy.17 = f32[32,3,512]{2,0,1:T(8,128)} copy(f32[32,3,512]{2,0,1:T(8,128)S(1)} %bitcast.15) | data formatting | bytes 393216
Async XLA Ops:
  0.6 2.9 %copy-start = (bf16[512,3,512]{2,0,1:T(8,128)(2,1)S(1)}, bf16[512,3,512]{2,0,1:T(8,128)(2,1)}, u32[]{:S(2)}) copy-start(bf16[512,3,512]{2,0,1:T(8,128)(2,1)} %param.13) | copy-start | bytes 4718596
  0.6 2.9 %copy-start.1 = (bf16[64,8,5,3]{0,1,3,2:T(8,128)(2,1)S(1)}, bf16[64,8,5,3]{0,1,3,2:T(8,128)(2,1)}, u32[]{:S(2)}) copy-start(bf16[64,8,5,3]{0,1,3,2:T(8,128)(2,1)} %param.11) | copy-start | bytes 46084
  0.7 2.9 %copy-start.2 = (f32[6,8,3]{1,2,0:T(4,128)S(1)}, f32[6,8,3]{1,2,0:T(4,128)}, u32[]{:S(2)}) copy-start(f32[6,8,3]{1,2,0:T(4,128)} %param.12) | copy-start | bytes 1732
  0.7 2.9 %copy-start.3 = (s32[64]{0:T(128)S(1)}, s32[64]{0:T(128)}, u32[]{:S(2)}) copy-start(s32[64]{0:T(128)} %param.9) | copy-start | bytes 772
  0.7 2.9 %copy-start.4 = (s32[64]{0:T(128)S(1)}, s32[64]{0:T(128)}, u32[]{:S(2)}) copy-start(s32[64]{0:T(128)} %param.10) | copy-start | bytes 772
